TPU v7x, 32 devices: a whole 2x2x4 slice. The times are simulated.
32 devices in a mesh: groups: 2 (over y), gx: 4 (over z), gy: 2 (over x), gz: 2 (over core).
Axes of the slice: x: 2, y: 2, z: 4, core: 2. Of those that a mesh axis runs over, the one named last changes fastest.
Arguments:
- positions: float32 [8, 2, 2, 3, 128], P(('groups', 'gx'), 'gy', 'gz'), parts along dimension 0, may hold values from 0 to 1
- species: int32 [8, 2, 2, 128], P(('groups', 'gx'), 'gy', 'gz'), parts along dimension 0, may hold values from 0 to 9
- atom_count: int32 [8, 2, 2, 1], P(('groups', 'gx'), 'gy', 'gz'), parts along dimension 0, may hold values from 64 to 128, as said below
- boundary: int32 [8, 2, 2, 32], P(('groups', 'gx'), 'gy', 'gz'), parts along dimension 0, may hold values from 0 to 127, as said below
- senders: int32 [8, 2, 2, 32, 128], P(('groups', 'gx'), 'gy', 'gz'), parts along dimension 0, may hold values from 0 to 991, as said below
- neighbour_count: int32 [8, 2, 2, 128], P(('groups', 'gx'), 'gy', 'gz'), parts along dimension 0, may hold values from 8 to 32, as said below
- embed: float32 [10, 128], replicated, may hold values from -6 to 6
- radial_first: float32 [2, 8, 64], replicated, may hold values from -2 to 2
- radial_second: float32 [2, 64, 128], replicated, may hold values from -0.75 to 0.75
- mix: float32 [2, 384, 128], replicated, may hold values from -0.3125 to 0.3125
- readout: float32 [128], replicated, may hold values from -0.5 to 0.5
Outputs:
- forces: float32 [8, 2, 2, 3, 128], P(('groups', 'gx'), 'gy', 'gz'), parts along dimension 0
- energy: float32 [2], P('groups'), parts along dimension 0
There are 2 independent parts, one for each index of `groups`. A program takes and returns all parts, laid end to end along the dimension named above; an argument that names none is the same for every part. Nothing has to cross between parts.
Inputs may be any that keep to these rules, and one draw needn't show every extreme that they name: `atom_count`: one brick in every draw holds 128 live atoms. `boundary`: each entry is below its brick's atom_count. `senders`: an own atom below its brick's atom_count, or 128 + slot * 32 + row with slot not 13. `neighbour_count`: every brick in every draw has an atom with all 32 slots live.
All inputs are finite; a program needn't handle non-finite values.
Results may differ from a plain program's by a relative error of at most 0.000082.
Values sent between devices are 32-bit elements; how exact they have to be, the bound alone decides.
A program may use at most 64 MiB of HBM per device.

v0:
```python
import functools
import itertools

import jax
import jax.numpy as jnp
from jax import lax
from jax.experimental import pallas as pl
from jax.experimental.pallas import tpu as pltpu
from jax.sharding import PartitionSpec as P

AXES = ("gx", "gy", "gz")
ATOMS, CH, NEIGH, RH, NB, RIM, NSPEC = 128, 128, 32, 64, 8, 32, 10
GROUP = 4
STEPS = NEIGH // GROUP
WIDE = GROUP * ATOMS
F32, BF16 = jnp.float32, jnp.bfloat16
NN = (((1,), (0,)), ((), ()))
NT = (((1,), (1,)), ((), ()))
TN = (((0,), (0,)), ((), ()))
R3, R5, R15 = 3.0**0.5, 5.0**0.5, 15.0**0.5
PI = 3.141592653589793


def split2(x):
    hi = x.astype(BF16).astype(F32)
    return hi, x - hi


def split3(x):
    a, rest = split2(x)
    b, c = split2(rest)
    return a, b, c


def mm(a, b, dims):
    return lax.dot_general(a.astype(BF16), b.astype(BF16), dims, preferred_element_type=F32)


def dot3(a, b, dims):
    ah, al = split2(a)
    bh, bl = split2(b)
    return mm(ah, bh, dims) + (mm(ah, bl, dims) + mm(al, bh, dims))


def sigmoid(x):
    return 1.0 / (1.0 + jnp.exp(-x))


def lanes(value, q):
    return value[:, q * ATOMS : (q + 1) * ATOMS]


def plan(sizes):
    counts = [2 if s == 2 else 3 for s in sizes]
    moves = []
    for code in itertools.product(*[range(c) for c in counts]):
        moves.append(tuple({0: 0, 1: 1, 2: s - 1}[c] for c, s in zip(code, sizes)))
    return counts, moves[1:]


def kernel(
    sizes,
    pos_ref, spec_ref, count_ref, bound_ref, send_ref, ncount_ref,
    emb_ref, w1_ref, w2_ref, mix_ref, read_ref,
    force_ref, energy_ref,
    geo, rimgeo, geoland, oh, rid, off, gsc, bsc, dbp, yref, geom,
    pre, rad, feat, msg, dens, inv, dd, dysum, dbsum, dg, dr, ddsc, empad,
    rimh, hland, gland, dtab, gtab, cland, ex, ey, ez, etile,
    geo_s, geo_r, h_s, h_r, g_s, g_r, c_s, c_r, ex_s, ex_r, ey_s, ey_r, ez_s, ez_r,
):
    counts, moves = plan(sizes)
    D = len(moves)
    K = oh.shape[1]
    me = [lax.axis_index(a) for a in AXES]

    def at(move, sign):
        return {
            a: lax.rem(m + (d if sign > 0 else s - d), s)
            for a, m, d, s in zip(AXES, me, move, sizes)
        }

    def remote(src, dst, s_sem, r_sem, where):
        return pltpu.make_async_remote_copy(
            src_ref=src, dst_ref=dst, send_sem=s_sem, recv_sem=r_sem,
            device_id=where, device_id_type=pl.DeviceIdType.MESH,
        )

    spare = hland.shape[0] - D * RIM
    if spare:
        hland[D * RIM :, :] = jnp.zeros((spare, CH), F32)
        gland[D * RIM :, :] = jnp.zeros((spare, CH), F32)

    partners = list(moves)
    for axis, s in enumerate(sizes):
        for d in range(1, s):
            move = tuple(d if i == axis else 0 for i in range(3))
            if move not in partners:
                partners.append(move)
    barrier = pltpu.get_barrier_semaphore()
    for move in partners:
        pl.semaphore_signal(barrier, inc=1, device_id=at(move, 1), device_id_type=pl.DeviceIdType.MESH)

    brow = bound_ref[0, 0]
    brow = jnp.concatenate([brow] * 4, axis=1)
    atom_row = lax.broadcasted_iota(jnp.int32, (ATOMS, ATOMS), 0)
    pick = (atom_row == brow).astype(F32)
    pick_t = pick.T
    coords = pos_ref[0, 0, 0]
    kinds = spec_ref[0, 0].astype(F32)
    geo[...] = jnp.zeros_like(geo)
    geo[0:3, :] = coords
    geo[3:4, :] = kinds
    own_geo = geo[...]
    g0, g1, g2 = split3(own_geo)
    rimgeo[...] = (mm(g0, pick, NN) + mm(g1, pick, NN)) + mm(g2, pick, NN)

    pl.semaphore_wait(barrier, len(partners))
    geo_copies = [
        remote(rimgeo, geoland.at[j], geo_s.at[j], geo_r.at[j], at(moves[j], -1)) for j in range(D)
    ]
    for c in geo_copies:
        c.start()

    s = send_ref[0, 0, 0]
    slot_index = lax.broadcasted_iota(jnp.int32, (NEIGH, ATOMS), 0)
    live = slot_index < ncount_ref[0, 0]
    ghost = s >= ATOMS
    t = jnp.where(ghost, s - ATOMS, 0)
    slot = lax.shift_right_logical(t, 5)
    row = t - slot * RIM
    one = lambda c: jnp.where(c, 1, 0)
    sx = one(slot >= 9) + one(slot >= 18)
    rem = slot - 9 * sx
    sy = one(rem >= 3) + one(rem >= 6)
    sz = rem - 3 * sy
    ident = jnp.zeros_like(s)
    for axis, (v, cnt) in enumerate(zip((sx, sy, sz), counts)):
        code = one(v != 1) if cnt == 2 else jnp.where(v == 0, 2, v - 1)
        ident = ident * cnt + code
        off[axis] = jnp.where(ghost, (v - 1).astype(F32), 0.0)
    rows = jnp.where(ghost, ATOMS + (ident - 1) * RIM + row, s)
    rid[...] = jnp.where(live, rows, -1)

    table_row = lax.broadcasted_iota(jnp.int32, (K, ATOMS), 0)

    def build(i, carry):
        for q in range(GROUP):
            r = rid[pl.ds(i * GROUP + q, 1), :]
            oh[i, :, q * ATOMS : (q + 1) * ATOMS] = jnp.where(table_row == r, 1.0, 0.0).astype(BF16)
        return carry

    lax.fori_loop(0, STEPS, build, 0)

    empad[...] = jnp.zeros_like(empad)
    empad[0:NSPEC, :] = emb_ref[...]
    eh, el = split2(empad[...])
    emb_cat = jnp.concatenate([eh, el], axis=0)
    spec_row = lax.broadcasted_iota(jnp.int32, (32, ATOMS), 0)
    spec_row = jnp.where(spec_row >= 16, spec_row - 16, spec_row).astype(F32)
    h0 = mm(emb_cat, (spec_row == kinds).astype(F32), TN)
    ddsc[...] = jnp.zeros_like(ddsc)
    readout = jnp.broadcast_to(read_ref[...], (ATOMS, CH)).T
    live_atoms = (
        lax.broadcasted_iota(jnp.int32, (CH, ATOMS), 1) < count_ref[0, 0]
    ).astype(F32)

    for c in geo_copies:
        c.wait()
    lane_block = lax.shift_right_logical(lax.broadcasted_iota(jnp.int32, (8, ATOMS), 1), 5)
    tiles = [own_geo]
    for tile in range(K // ATOMS - 1):
        value = jnp.zeros((8, ATOMS), F32)
        for b in range(4):
            if tile * 4 + b < D:
                value = jnp.where(lane_block == b, geoland[tile * 4 + b], value)
        tiles.append(value)
    table_geo = jnp.concatenate(split3(jnp.concatenate(tiles, axis=1)), axis=0).astype(BF16)

    def gather_geo(i, carry):
        x = lax.dot_general(table_geo, oh[i], NN, preferred_element_type=F32)
        x = (x[0:8] + x[8:16]) + x[16:24]
        for q in range(GROUP):
            gsc[i * GROUP + q] = lanes(x, q)
        return carry

    lax.fori_loop(0, STEPS, gather_geo, 0)

    deltas = [(gsc[:, a, :] + off[a]) - coords[a : a + 1, :] for a in range(3)]
    dist = jnp.sqrt(deltas[0] * deltas[0] + deltas[1] * deltas[1] + deltas[2] * deltas[2] + 0.25)
    rinv = 1.0 / dist
    ux, uy, uz = (d * rinv for d in deltas)
    geom[0], geom[1], geom[2], geom[3] = ux, uy, uz, rinv
    ylm = [
        None, R3 * ux, R3 * uy, R3 * uz,
        R15 * ux * uy, R15 * uy * uz, R15 * uz * ux,
        (0.5 * R15) * (ux * ux - uy * uy), (0.5 * R5) * (3.0 * uz * uz - 1.0),
    ]
    for k in range(1, 9):
        yref[k] = ylm[k]
    q4 = dist * 0.25
    inner = 1.0 - q4 * q4
    env = inner * inner * rinv
    denv = -(inner * q4 + env) * rinv
    s1, c1 = jnp.sin(PI * q4), jnp.cos(PI * q4)
    sm, cm, sp, cp = s1, c1, jnp.zeros_like(s1), jnp.ones_like(s1)
    for m in range(NB):
        bsc[:, m, :] = sm * env
        dbp[m] = ((m + 1) * PI * 0.25) * cm * env + sm * denv
        sm, sp = 2.0 * c1 * sm - sp, sm
        cm, cp = 2.0 * c1 * cm - cp, cm
    kind_edge = gsc[:, 3, :]
    rid_kind = jnp.where(live, kind_edge, -1.0)
    geom[4] = rid_kind

    def radial(layer, with_feat):
        w1h, w1l = split2(w1_ref[layer])
        w1c = jnp.concatenate([w1h, w1h, w1l], axis=0).astype(BF16)
        w2h, w2l = split2(w2_ref[layer])
        w2c = jnp.concatenate([w2h, w2h, w2l], axis=0).astype(BF16)

        def step(i, carry):
            b = jnp.concatenate([bsc[i * GROUP + q] for q in range(GROUP)], axis=1)
            bh, bl = split2(b)
            bc = jnp.concatenate([bh, bl, bh], axis=0).astype(BF16)
            p = lax.dot_general(w1c, bc, TN, preferred_element_type=F32)
            pre[layer, i] = p
            hid = p * sigmoid(p)
            hh, hl = split2(hid)
            hc = jnp.concatenate([hh, hl, hh], axis=0).astype(BF16)
            r = lax.dot_general(w2c, hc, TN, preferred_element_type=F32)
            rad[i] = r
            if with_feat:
                for q in range(GROUP):
                    kind = geom[4, pl.ds(i * GROUP + q, 1), :]
                    f = mm(emb_cat, (spec_row == kind).astype(F32), TN)
                    feat[layer, i, :, q * ATOMS : (q + 1) * ATOMS] = f
                    msg[layer, i, :, q * ATOMS : (q + 1) * ATOMS] = f * lanes(r, q)
            return carry

        lax.fori_loop(0, STEPS, step, 0)

    def density(layer):
        def step(cb, carry):
            at_rows = pl.ds(pl.multiple_of(cb * 16, 16), 16)
            acc = [None] * 9
            for n in range(NEIGH):
                lo = (n % GROUP) * ATOMS
                m = msg[layer, n // GROUP, at_rows, lo : lo + ATOMS]
                for k in range(9):
                    term = m if k == 0 else m * yref[k, n : n + 1, :]
                    acc[k] = term if n == 0 else acc[k] + term
            acc = [a * (1.0 / NEIGH) for a in acc]
            for k in range(9):
                dens[k, at_rows, :] = acc[k]
            inv[0, at_rows, :] = acc[0]
            inv[1, at_rows, :] = acc[1] * acc[1] + acc[2] * acc[2] + acc[3] * acc[3]
            sq = acc[4] * acc[4]
            for k in range(5, 9):
                sq = sq + acc[k] * acc[k]
            inv[2, at_rows, :] = sq
            return carry

        lax.fori_loop(0, CH // 16, step, 0)
        z = None
        for part in range(3):
            term = dot3(mix_ref[layer, part * CH : (part + 1) * CH, :], inv[part], TN)
            z = term if z is None else z + term
        return z

    def density_grad(layer, dz):
        for part in range(3):
            d = dot3(mix_ref[layer, part * CH : (part + 1) * CH, :], dz, NN)
            if part == 0:
                dd[0] = d * (1.0 / NEIGH)
            else:
                d = d * (2.0 / NEIGH)
                for k in range(1, 4) if part == 1 else range(4, 9):
                    dd[k] = d * dens[k]

    radial(0, True)
    z1 = density(0)
    sig1 = sigmoid(z1)
    h1 = h0 + z1 * sig1
    dz1 = sig1 * (1.0 + z1 * (1.0 - sig1))
    first = [dens[k] for k in range(1, 9)]
    for k in range(1, 9):
        dd[9 + k] = first[k - 1]

    hh, hl = split2(h1)
    rimh[...] = mm(pick_t[0:RIM], hh, NT) + mm(pick_t[0:RIM], hl, NT)
    h_copies = [
        remote(rimh, hland.at[pl.ds(j * RIM, RIM)], h_s.at[j], h_r.at[j], at(moves[j], -1))
        for j in range(D)
    ]
    for c in h_copies:
        c.start()
    radial(1, False)
    for c in h_copies:
        c.wait()

    parts_t = [h1] + [hland[u * ATOMS : (u + 1) * ATOMS, :].T for u in range(K // ATOMS - 1)]
    table_h = jnp.concatenate(split2(jnp.concatenate(parts_t, axis=1)), axis=0).astype(BF16)

    def gather_h(i, carry):
        x = lax.dot_general(table_h, oh[i], NN, preferred_element_type=F32)
        f = x[0:CH] + x[CH : 2 * CH]
        feat[1, i] = f
        msg[1, i] = f * rad[i]
        return carry

    lax.fori_loop(0, STEPS, gather_h, 0)
    z2 = density(1)
    sig2 = sigmoid(z2)
    final = h1 + z2 * sig2
    sigf = sigmoid(final)
    weight = readout * live_atoms
    contrib = weight * (final * sigf)
    part = contrib[0:8]
    for u in range(1, CH // 8):
        part = part + contrib[u * 8 : (u + 1) * 8]

    def spread(axis, land, s_sem, r_sem, value):
        size = sizes[axis]
        mine = me[axis]
        land[mine] = value
        copies = []
        for d in range(1, size):
            move = tuple(d if i == axis else 0 for i in range(3))
            copies.append(remote(land.at[mine], land.at[mine], s_sem.at[d], r_sem.at[d], at(move, 1)))
        for c in copies:
            c.start()
        return copies

    def gathered(axis, land, copies):
        for c in copies:
            c.wait()
        total = land[0]
        for i in range(1, sizes[axis]):
            total = total + land[i]
        return total

    e_copies = spread(0, ex, ex_s, ex_r, part)

    dfinal = weight * (sigf * (1.0 + final * (1.0 - sigf)))
    density_grad(1, dfinal * (sig2 * (1.0 + z2 * (1.0 - sig2))))

    def back_feat(i, carry):
        for q in range(GROUP):
            cut = slice(q * ATOMS, (q + 1) * ATOMS)
            dm = dd[0]
            for k in range(1, 9):
                dm = dm + yref[k, pl.ds(i * GROUP + q, 1), :] * dd[k]
            gh, gl = split2(dm * rad[i, :, cut])
            dg[i, 0:CH, cut] = gh.astype(BF16)
            dg[i, CH : 2 * CH, cut] = gl.astype(BF16)
            dr[i, :, cut] = dm * feat[1, i, :, cut]
        return carry

    lax.fori_loop(0, STEPS, back_feat, 0)

    dtab[...] = jnp.zeros_like(dtab)

    def scatter_h(i, carry):
        dtab[...] += lax.dot_general(oh[i], dg[i], NT, preferred_element_type=F32)
        return carry

    lax.fori_loop(0, STEPS, scatter_h, 0)
    gtab[...] = dtab[:, 0:CH] + dtab[:, CH : 2 * CH]
    g_copies = [
        remote(
            gtab.at[pl.ds(ATOMS + j * RIM, RIM)], gland.at[pl.ds(j * RIM, RIM)],
            g_s.at[j], g_r.at[j], at(moves[j], 1),
        )
        for j in range(D)
    ]
    for c in g_copies:
        c.start()
    own_dh = gtab[0:ATOMS, :].T

    def back_radial(layer, first_pass):
        w1h, w1l = split2(w1_ref[layer])
        w2h, w2l = split2(w2_ref[layer])
        w2c = jnp.concatenate([w2h, w2h, w2l], axis=1).astype(BF16)

        def step(i, carry):
            v = dr[i]
            vh, vl = split2(v)
            vc = jnp.concatenate([vh, vl, vh], axis=0).astype(BF16)
            dhid = lax.dot_general(w2c, vc, NN, preferred_element_type=F32)
            p = pre[layer, i]
            sg = sigmoid(p)
            dp = dhid * (sg * (1.0 + p * (1.0 - sg)))
            ph, p_lo = split2(dp)
            db = mm(w1h, ph, NN) + (mm(w1h, p_lo, NN) + mm(w1l, ph, NN))
            for q in range(GROUP):
                if first_pass:
                    dbsum[i * GROUP + q] = lanes(db, q)
                else:
                    dbsum[i * GROUP + q] += lanes(db, q)
            return carry

        lax.fori_loop(0, STEPS, step, 0)

    def back_sphere(i, carry):
        for q in range(GROUP):
            cut = slice(q * ATOMS, (q + 1) * ATOMS)
            m = msg[1, i, :, cut]
            for k in range(1, 9):
                dysum[k, pl.ds(i * GROUP + q, 1), :] = jnp.sum(m * dd[k], axis=0, keepdims=True)
        return carry

    lax.fori_loop(0, STEPS, back_sphere, 0)
    back_radial(1, True)
    part = gathered(0, ex, e_copies)
    e_copies = spread(1, ey, ey_s, ey_r, part)

    for c in g_copies:
        c.wait()
    back = gland[0:ATOMS, :]
    for u in range(1, gland.shape[0] // ATOMS):
        back = back + gland[u * ATOMS : (u + 1) * ATOMS, :]
    bh, bl = split2(back.T)
    dh1 = dfinal + own_dh + (mm(bh, pick, NT) + mm(bl, pick, NT))
    for k in range(1, 9):
        dens[k] = dd[9 + k]
    density_grad(0, dh1 * dz1)

    def back_first(i, carry):
        for q in range(GROUP):
            cut = slice(q * ATOMS, (q + 1) * ATOMS)
            m = msg[0, i, :, cut]
            dm = dd[0]
            for k in range(1, 9):
                at_n = pl.ds(i * GROUP + q, 1)
                g = dd[k]
                dm = dm + yref[k, at_n, :] * g
                dysum[k, at_n, :] += jnp.sum(m * g, axis=0, keepdims=True)
            dr[i, :, cut] = dm * feat[0, i, :, cut]
        return carry

    lax.fori_loop(0, STEPS, back_first, 0)
    back_radial(0, False)
    part = gathered(1, ey, e_copies)
    e_copies = spread(2, ez, ez_s, ez_r, part)

    ux, uy, uz, rinv = geom[0], geom[1], geom[2], geom[3]
    dy = [None] + [dysum[k] for k in range(1, 9)]
    gx = R3 * dy[1] + R15 * (uy * dy[4] + uz * dy[6] + ux * dy[7])
    gy = R3 * dy[2] + R15 * (ux * dy[4] + uz * dy[5] - uy * dy[7])
    gz = R3 * dy[3] + R15 * (uy * dy[5] + ux * dy[6]) + (3.0 * R5) * uz * dy[8]
    drad = dbsum[:, 0, :] * dbp[0]
    for m in range(1, NB):
        drad = drad + dbsum[:, m, :] * dbp[m]
    drad = drad - (gx * ux + gy * uy + gz * uz) * rinv
    centre = []
    for a, (g, u) in enumerate(((gx, ux), (gy, uy), (gz, uz))):
        d = jnp.where(live, g * rinv + u * drad, 0.0)
        ddsc[:, a, :] = d
        centre.append(jnp.sum(d, axis=0, keepdims=True))

    def scatter_geo(i, carry):
        d = jnp.concatenate([ddsc[i * GROUP + q] for q in range(GROUP)], axis=1)
        d = jnp.concatenate(split2(d), axis=0).astype(BF16)
        return carry + lax.dot_general(d, oh[i], NT, preferred_element_type=F32)

    dxyz = lax.fori_loop(0, STEPS, scatter_geo, jnp.zeros((16, K), F32))
    dxyz = dxyz[0:8] + dxyz[8:16]
    for u in range(K // ATOMS):
        etile[u] = lanes(dxyz, u)
    c_copies = [
        remote(etile.at[1 + j // 4], cland.at[j], c_s.at[j], c_r.at[j], at(moves[j], 1))
        for j in range(D)
    ]
    for c in c_copies:
        c.start()
    part = gathered(2, ez, e_copies)
    slots = float(ATOMS * sizes[0] * sizes[1] * sizes[2])
    energy_ref[...] = jnp.broadcast_to(jnp.sum(part) / slots, energy_ref.shape)
    for c in c_copies:
        c.wait()
    ret = jnp.zeros((8, ATOMS), F32)
    for j in range(D):
        ret = ret + jnp.where(lane_block == j % 4, cland[j], 0.0)
    r0, r1 = split2(ret)
    grad = etile[0] + (mm(r0, pick, NT) + mm(r1, pick, NT))
    for a in range(3):
        force_ref[0, 0, 0, a : a + 1, :] = centre[a] - grad[a : a + 1, :]


def on_device(
    sizes, positions, species, atom_count, boundary, senders, neighbour_count,
    embed, radial_first, radial_second, mix, readout,
):
    _, moves = plan(sizes)
    D = len(moves)
    T = -(-D * RIM // ATOMS)
    K = ATOMS * (1 + T)
    vm = pltpu.VMEM
    dma = pltpu.SemaphoreType.DMA
    scratch = [
        vm((8, ATOMS), F32),
        vm((8, ATOMS), F32),
        vm((D, 8, ATOMS), F32),
        vm((STEPS, K, WIDE), BF16),
        vm((NEIGH, ATOMS), jnp.int32),
        vm((3, NEIGH, ATOMS), F32),
        vm((NEIGH, 8, ATOMS), F32),
        vm((NEIGH, NB, ATOMS), F32),
        vm((NB, NEIGH, ATOMS), F32),
        vm((9, NEIGH, ATOMS), F32),
        vm((5, NEIGH, ATOMS), F32),
        vm((2, STEPS, RH, WIDE), F32),
        vm((STEPS, CH, WIDE), F32),
        vm((2, STEPS, CH, WIDE), F32),
        vm((2, STEPS, CH, WIDE), F32),
        vm((9, CH, ATOMS), F32),
        vm((3, CH, ATOMS), F32),
        vm((18, CH, ATOMS), F32),
        vm((9, NEIGH, ATOMS), F32),
        vm((NEIGH, NB, ATOMS), F32),
        vm((STEPS, 2 * CH, WIDE), BF16),
        vm((STEPS, CH, WIDE), F32),
        vm((NEIGH, 8, ATOMS), F32),
        vm((16, CH), F32),
        vm((RIM, CH), F32),
        vm((T * ATOMS, CH), F32),
        vm((T * ATOMS, CH), F32),
        vm((K, 2 * CH), F32),
        vm((K, CH), F32),
        vm((D, 8, ATOMS), F32),
        vm((sizes[0], 8, ATOMS), F32),
        vm((sizes[1], 8, ATOMS), F32),
        vm((sizes[2], 8, ATOMS), F32),
        vm((1 + T, 8, ATOMS), F32),
    ]
    for amount in (D, D, D, D, sizes[0], sizes[1], sizes[2]):
        scratch += [dma((amount,)), dma((amount,))]
    forces, energy = pl.pallas_call(
        functools.partial(kernel, sizes),
        out_shape=(
            jax.ShapeDtypeStruct((1, 1, 1, 3, ATOMS), F32),
            jax.ShapeDtypeStruct((1, ATOMS), F32),
        ),
        in_specs=[pl.BlockSpec(memory_space=pltpu.VMEM)] * 11,
        out_specs=(pl.BlockSpec(memory_space=pltpu.VMEM),) * 2,
        scratch_shapes=scratch,
        compiler_params=pltpu.CompilerParams(
            collective_id=0, has_side_effects=True, vmem_limit_bytes=50 * 1024 * 1024
        ),
        name="brick",
    )(
        positions, species.reshape(1, 1, 1, ATOMS), atom_count.reshape(1, 1, 1, 1),
        boundary.reshape(1, 1, 1, RIM), senders, neighbour_count.reshape(1, 1, 1, ATOMS),
        embed, radial_first, radial_second, mix, readout.reshape(1, CH),
    )
    return forces, energy[0, 0:1]


def solution(mesh):
    sizes = tuple(mesh.shape[a] for a in AXES)
    brick = lambda extra: P(("groups", "gx"), "gy", "gz", *([None] * extra))
    in_specs = (brick(2), brick(1), brick(1), brick(1), brick(2), brick(1), P(), P(), P(), P(), P())
    return jax.shard_map(
        functools.partial(on_device, sizes),
        mesh=mesh,
        in_specs=in_specs,
        out_specs=(brick(2), P("groups")),
        check_vma=False,
    )
```

profile of v0, /device:TPU:0, one launch (start us, length us, event | category | flops | bytes accessed | tf_op | source)
XLA Modules:
  0.0 60.3 jit_solution(7067754156827866571)
XLA Ops:
  0.6 0.0 copy-start.9
  1.3 0.0 copy-done.9
  1.3 0.0 copy-start.5
  1.3 0.0 copy-start.6
  1.3 0.0 copy-start.7
  1.3 0.0 copy-start.8
  1.4 0.6 %copy-done.5 = s32[1,1,1,128]{3,2,1,0:T(1,128)S(1)} copy-done((s32[1,1,1,128]{3,2,1,0:T(1,128)S(1)}, s32[1,1,1,128]{3,2,1,0:T(1,128)}, u32[]{:S(2)}) %copy-start.5) | copy-done | bytes 536
  2.0 0.0 copy-done.6
  2.0 0.0 copy-done.7
  2.0 0.0 copy-done.8
  2.0 0.0 copy-start
  2.0 1.0 %copy-done = f32[2,384,128]{2,1,0:T(8,128)S(1)} copy-done((f32[2,384,128]{2,1,0:T(8,128)S(1)}, f32[2,384,128]{2,1,0:T(8,128)}, u32[]{:S(2)}) %copy-start) | copy-done | bytes 393240
  3.0 0.0 copy-start.1
  3.0 0.8 %copy-done.1 = f32[2,64,128]{2,1,0:T(8,128)S(1)} copy-done((f32[2,64,128]{2,1,0:T(8,128)S(1)}, f32[2,64,128]{2,1,0:T(8,128)}, u32[]{:S(2)}) %copy-start.1) | copy-done | bytes 65560
  3.9 0.0 copy-start.2
  3.9 0.7 %copy-done.2 = s32[1,1,1,32,128]{4,3,2,1,0:T(8,128)S(1)} copy-done((s32[1,1,1,32,128]{4,3,2,1,0:T(8,128)S(1)}, s32[1,1,1,32,128]{4,3,2,1,0:T(8,128)}, u32[]{:S(2)}) %copy-start.2) | copy-done | bytes 16408
  4.6 0.0 copy-start.3
  4.6 0.7 %copy-done.3 = f32[10,128]{1,0:T(8,128)S(1)} copy-done((f32[10,128]{1,0:T(8,128)S(1)}, f32[10,128]{1,0:T(8,128)}, u32[]{:S(2)}) %copy-start.3) | copy-done | bytes 5144
  5.3 0.0 copy-start.4
  5.3 0.7 %copy-done.4 = f32[2,8,64]{2,1,0:T(8,128)S(1)} copy-done((f32[2,8,64]{2,1,0:T(8,128)S(1)}, f32[2,8,64]{2,1,0:T(8,128)}, u32[]{:S(2)}) %copy-start.4) | copy-done | bytes 4120
  6.0 52.6 %brick.1 = (f32[1,1,1,3,128]{4,3,2,1,0:T(4,128)S(1)}, f32[1,128]{1,0:T(1,128)S(1)}) custom-call(f32[1,1,1,3,128]{4,3,2,1,0:T(4,128)S(1)} %copy.13.pos_ref, s32[1,1,1,128]{3,2,1,0:T(1,128)S(1)} %copy-done.5, s32[1,1,1,1]{3,2,1,0:T(1,128)S(6)} %copy.16.count_ref, s32[1,1,1,32]{3,2,1,0:T(1,128)S(1)} %copy-done.6, s32[1,1,1,32,128]{4,3,2,1,0:T(8,128)S(1)} %copy-done.2, ...), custom_call_target="tpu_custom_call" | custom-call | tf_op jit(solution)/shard_map/brick/pallas_call | solution.py:538
  58.6 0.6 copy.14
  (1 shorter events, 0.0 us)
Async XLA Ops:
  0.6 0.7 %copy-start.9 = (f32[1,1,1,3,128]{4,2,3,1,0:T(1,128)S(1)}, f32[1,1,1,3,128]{4,2,3,1,0:T(1,128)}, u32[]{:S(2)}) copy-start(f32[1,1,1,3,128]{4,2,3,1,0:T(1,128)} %param.11) | copy-start | bytes 4612
  1.3 0.7 %copy-start.5 = (s32[1,1,1,128]{3,2,1,0:T(1,128)S(1)}, s32[1,1,1,128]{3,2,1,0:T(1,128)}, u32[]{:S(2)}) copy-start(s32[1,1,1,128]{3,2,1,0:T(1,128)} %spec_ref.1) | copy-start | bytes 1540
  1.3 0.7 %copy-start.6 = (s32[1,1,1,32]{3,2,1,0:T(1,128)S(1)}, s32[1,1,1,32]{3,2,1,0:T(1,128)}, u32[]{:S(2)}) copy-start(s32[1,1,1,32]{3,2,1,0:T(1,128)} %bound_ref.1) | copy-start | bytes 388
  1.3 0.7 %copy-start.7 = (s32[1,1,1,128]{3,2,1,0:T(1,128)S(1)}, s32[1,1,1,128]{3,2,1,0:T(1,128)}, u32[]{:S(2)}) copy-start(s32[1,1,1,128]{3,2,1,0:T(1,128)} %ncount_ref.1) | copy-start | bytes 1540
  1.3 0.7 %copy-start.8 = (f32[128]{0:T(128)S(1)}, f32[128]{0:T(128)}, u32[]{:S(2)}) copy-start(f32[128]{0:T(128)} %param.21) | copy-start | bytes 1540
  2.0 1.0 %copy-start = (f32[2,384,128]{2,1,0:T(8,128)S(1)}, f32[2,384,128]{2,1,0:T(8,128)}, u32[]{:S(2)}) copy-start(f32[2,384,128]{2,1,0:T(8,128)} %mix_ref.1) | copy-start | bytes 1179652
  3.0 0.8 %copy-start.1 = (f32[2,64,128]{2,1,0:T(8,128)S(1)}, f32[2,64,128]{2,1,0:T(8,128)}, u32[]{:S(2)}) copy-start(f32[2,64,128]{2,1,0:T(8,128)} %w2_ref.1) | copy-start | bytes 196612
  3.9 0.7 %copy-start.2 = (s32[1,1,1,32,128]{4,3,2,1,0:T(8,128)S(1)}, s32[1,1,1,32,128]{4,3,2,1,0:T(8,128)}, u32[]{:S(2)}) copy-start(s32[1,1,1,32,128]{4,3,2,1,0:T(8,128)} %send_ref.1) | copy-start | bytes 49156
  4.6 0.7 %copy-start.3 = (f32[10,128]{1,0:T(8,128)S(1)}, f32[10,128]{1,0:T(8,128)}, u32[]{:S(2)}) copy-start(f32[10,128]{1,0:T(8,128)} %emb_ref.1) | copy-start | bytes 15364
  5.3 0.7 %copy-start.4 = (f32[2,8,64]{2,1,0:T(8,128)S(1)}, f32[2,8,64]{2,1,0:T(8,128)}, u32[]{:S(2)}) copy-start(f32[2,8,64]{2,1,0:T(8,128)} %w1_ref.1) | copy-start | bytes 12292
where the time goes:
time: 60.7 us; the launch traced here: 60.3 us
  Pallas kernels  52.6 us (87%)
  local copies, waits for them, and re-layouts  5.19 us (9%)
  between operations  2.52 us (4%)
    pallas_call x1, Pallas kernels, on_device(): pl.pallas_call(functools.partial(kernel, sizes), out_shape=(jax.ShapeDtyp...  52.6 us
    unnamed x22, local copies, waits for them, and re-layouts  5.19 us

commit v1 on v0

--- a/solution.py
+++ b/solution.py
@@ -55,22 +55,33 @@
     moves = []
     for code in itertools.product(*[range(c) for c in counts]):
         moves.append(tuple({0: 0, 1: 1, 2: s - 1}[c] for c, s in zip(code, sizes)))
-    return counts, moves[1:]
+    return counts, moves[:0:-1]
 
 
 def kernel(
     sizes,
-    pos_ref, spec_ref, count_ref, bound_ref, send_ref, ncount_ref,
-    emb_ref, w1_ref, w2_ref, mix_ref, read_ref,
+    pos_any, spec_any, count_any, bound_any, send_any, ncount_any,
+    emb_any, w1_any, w2_any, mix_any, read_any,
     force_ref, energy_ref,
     geo, rimgeo, geoland, oh, rid, off, gsc, bsc, dbp, yref, geom,
     pre, rad, feat, msg, dens, inv, dd, dysum, dbsum, dg, dr, ddsc, empad,
     rimh, hland, gland, dtab, gtab, cland, ex, ey, ez, etile,
+    pos_ref, spec_ref, count_ref, bound_ref, send_ref, ncount_ref,
+    emb_ref, w1_ref, w2_ref, mix_ref, read_ref, in_s,
     geo_s, geo_r, h_s, h_r, g_s, g_r, c_s, c_r, ex_s, ex_r, ey_s, ey_r, ez_s, ez_r,
 ):
     counts, moves = plan(sizes)
     D = len(moves)
     K = oh.shape[1]
+    loads = {}
+    for index, (name, src, dst) in enumerate((
+        ("bound", bound_any, bound_ref), ("pos", pos_any, pos_ref), ("spec", spec_any, spec_ref),
+        ("send", send_any, send_ref), ("ncount", ncount_any, ncount_ref), ("count", count_any, count_ref),
+        ("emb", emb_any, emb_ref), ("w1", w1_any, w1_ref), ("w2", w2_any, w2_ref),
+        ("read", read_any, read_ref), ("mix", mix_any, mix_ref),
+    )):
+        loads[name] = pltpu.make_async_copy(src, dst, in_s.at[index])
+        loads[name].start()
     me = [lax.axis_index(a) for a in AXES]
 
     def at(move, sign):
@@ -100,6 +111,8 @@
     for move in partners:
         pl.semaphore_signal(barrier, inc=1, device_id=at(move, 1), device_id_type=pl.DeviceIdType.MESH)
 
+    for name in ("bound", "pos", "spec"):
+        loads[name].wait()
     brow = bound_ref[0, 0]
     brow = jnp.concatenate([brow] * 4, axis=1)
     atom_row = lax.broadcasted_iota(jnp.int32, (ATOMS, ATOMS), 0)
@@ -121,6 +134,8 @@
     for c in geo_copies:
         c.start()
 
+    for name in ("send", "ncount"):
+        loads[name].wait()
     s = send_ref[0, 0, 0]
     slot_index = lax.broadcasted_iota(jnp.int32, (NEIGH, ATOMS), 0)
     live = slot_index < ncount_ref[0, 0]
@@ -138,7 +153,7 @@
         code = one(v != 1) if cnt == 2 else jnp.where(v == 0, 2, v - 1)
         ident = ident * cnt + code
         off[axis] = jnp.where(ghost, (v - 1).astype(F32), 0.0)
-    rows = jnp.where(ghost, ATOMS + (ident - 1) * RIM + row, s)
+    rows = jnp.where(ghost, ATOMS + (D - ident) * RIM + row, s)
     rid[...] = jnp.where(live, rows, -1)
 
     table_row = lax.broadcasted_iota(jnp.int32, (K, ATOMS), 0)
@@ -151,6 +166,8 @@
 
     lax.fori_loop(0, STEPS, build, 0)
 
+    for name in ("emb", "w1", "w2", "count", "read", "mix"):
+        loads[name].wait()
     empad[...] = jnp.zeros_like(empad)
     empad[0:NSPEC, :] = emb_ref[...]
     eh, el = split2(empad[...])
@@ -533,6 +550,12 @@
         vm((sizes[2], 8, ATOMS), F32),
         vm((1 + T, 8, ATOMS), F32),
     ]
+    operands = (
+        positions, species.reshape(1, 1, 1, ATOMS), atom_count.reshape(1, 1, 1, 1),
+        boundary.reshape(1, 1, 1, RIM), senders, neighbour_count.reshape(1, 1, 1, ATOMS),
+        embed, radial_first, radial_second, mix, readout.reshape(1, CH),
+    )
+    scratch += [vm(x.shape, x.dtype) for x in operands] + [dma((len(operands),))]
     for amount in (D, D, D, D, sizes[0], sizes[1], sizes[2]):
         scratch += [dma((amount,)), dma((amount,))]
     forces, energy = pl.pallas_call(
@@ -541,18 +564,14 @@
             jax.ShapeDtypeStruct((1, 1, 1, 3, ATOMS), F32),
             jax.ShapeDtypeStruct((1, ATOMS), F32),
         ),
-        in_specs=[pl.BlockSpec(memory_space=pltpu.VMEM)] * 11,
+        in_specs=[pl.BlockSpec(memory_space=pltpu.HBM)] * 11,
         out_specs=(pl.BlockSpec(memory_space=pltpu.VMEM),) * 2,
         scratch_shapes=scratch,
         compiler_params=pltpu.CompilerParams(
             collective_id=0, has_side_effects=True, vmem_limit_bytes=50 * 1024 * 1024
         ),
         name="brick",
-    )(
-        positions, species.reshape(1, 1, 1, ATOMS), atom_count.reshape(1, 1, 1, 1),
-        boundary.reshape(1, 1, 1, RIM), senders, neighbour_count.reshape(1, 1, 1, ATOMS),
-        embed, radial_first, radial_second, mix, readout.reshape(1, CH),
-    )
+    )(*operands)
     return forces, energy[0, 0:1]
 
 

time: 60.7 us -> 58.7 us (0.967)
  Pallas kernels: 52.6 us -> 50.6 us
    pallas_call x1, Pallas kernels: 52.6 us -> 50.6 us  [on_device(): pl.pallas_call(functools.partial(kernel, sizes), out_shape=(jax.ShapeDtyp...]
where the time goes in v1:
time: 58.7 us; the launch traced here: 58.3 us
  Pallas kernels  50.6 us (86%)
  local copies, waits for them, and re-layouts  5.19 us (9%)
  between operations  2.52 us (4%)
    pallas_call x1, Pallas kernels, on_device(): pl.pallas_call(functools.partial(kernel, sizes), out_shape=(jax.ShapeDtyp...  50.6 us
    unnamed x22, local copies, waits for them, and re-layouts  5.19 us

profile of v1, /device:TPU:0, one launch (start us, length us, event | category | flops | bytes accessed | tf_op | source)
XLA Modules:
  0.0 58.3 jit_solution(7414779340599385561)
XLA Ops:
  0.6 0.0 copy-start.9
  1.3 0.0 copy-done.9
  1.3 0.0 copy-start.5
  1.3 0.0 copy-start.6
  1.3 0.0 copy-start.7
  1.3 0.0 copy-start.8
  1.4 0.6 %copy-done.5 = s32[1,1,1,128]{3,2,1,0:T(1,128)S(1)} copy-done((s32[1,1,1,128]{3,2,1,0:T(1,128)S(1)}, s32[1,1,1,128]{3,2,1,0:T(1,128)}, u32[]{:S(2)}) %copy-start.5) | copy-done | bytes 536
  2.0 0.0 copy-done.6
  2.0 0.0 copy-done.7
  2.0 0.0 copy-done.8
  2.0 0.0 copy-start
  2.0 1.0 %copy-done = f32[2,384,128]{2,1,0:T(8,128)S(1)} copy-done((f32[2,384,128]{2,1,0:T(8,128)S(1)}, f32[2,384,128]{2,1,0:T(8,128)}, u32[]{:S(2)}) %copy-start) | copy-done | bytes 393240
  3.0 0.0 copy-start.1
  3.0 0.8 %copy-done.1 = f32[2,64,128]{2,1,0:T(8,128)S(1)} copy-done((f32[2,64,128]{2,1,0:T(8,128)S(1)}, f32[2,64,128]{2,1,0:T(8,128)}, u32[]{:S(2)}) %copy-start.1) | copy-done | bytes 65560
  3.9 0.0 copy-start.2
  3.9 0.7 %copy-done.2 = s32[1,1,1,32,128]{4,3,2,1,0:T(8,128)S(1)} copy-done((s32[1,1,1,32,128]{4,3,2,1,0:T(8,128)S(1)}, s32[1,1,1,32,128]{4,3,2,1,0:T(8,128)}, u32[]{:S(2)}) %copy-start.2) | copy-done | bytes 16408
  4.6 0.0 copy-start.3
  4.6 0.7 %copy-done.3 = f32[10,128]{1,0:T(8,128)S(1)} copy-done((f32[10,128]{1,0:T(8,128)S(1)}, f32[10,128]{1,0:T(8,128)}, u32[]{:S(2)}) %copy-start.3) | copy-done | bytes 5144
  5.3 0.0 copy-start.4
  5.3 0.7 %copy-done.4 = f32[2,8,64]{2,1,0:T(8,128)S(1)} copy-done((f32[2,8,64]{2,1,0:T(8,128)S(1)}, f32[2,8,64]{2,1,0:T(8,128)}, u32[]{:S(2)}) %copy-start.4) | copy-done | bytes 4120
  6.0 50.6 %brick.1 = (f32[1,1,1,3,128]{4,3,2,1,0:T(4,128)S(1)}, f32[1,128]{1,0:T(1,128)S(1)}) custom-call(f32[1,1,1,3,128]{4,3,2,1,0:T(4,128)S(1)} %copy.13.pos_any, s32[1,1,1,128]{3,2,1,0:T(1,128)S(1)} %copy-done.5, s32[1,1,1,1]{3,2,1,0:T(1,128)S(6)} %copy.16.count_any, s32[1,1,1,32]{3,2,1,0:T(1,128)S(1)} %copy-done.6, s32[1,1,1,32,128]{4,3,2,1,0:T(8,128)S(1)} %copy-done.2, ...), custom_call_target="tpu_custom_call" | custom-call | tf_op jit(solution)/shard_map/brick/pallas_call | solution.py:561
  56.6 0.6 copy.14
  (1 shorter events, 0.0 us)
Async XLA Ops:
  0.6 0.7 %copy-start.9 = (f32[1,1,1,3,128]{4,2,3,1,0:T(1,128)S(1)}, f32[1,1,1,3,128]{4,2,3,1,0:T(1,128)}, u32[]{:S(2)}) copy-start(f32[1,1,1,3,128]{4,2,3,1,0:T(1,128)} %param.11) | copy-start | bytes 4612
  1.3 0.7 %copy-start.5 = (s32[1,1,1,128]{3,2,1,0:T(1,128)S(1)}, s32[1,1,1,128]{3,2,1,0:T(1,128)}, u32[]{:S(2)}) copy-start(s32[1,1,1,128]{3,2,1,0:T(1,128)} %spec_any.1) | copy-start | bytes 1540
  1.3 0.7 %copy-start.6 = (s32[1,1,1,32]{3,2,1,0:T(1,128)S(1)}, s32[1,1,1,32]{3,2,1,0:T(1,128)}, u32[]{:S(2)}) copy-start(s32[1,1,1,32]{3,2,1,0:T(1,128)} %bound_any.1) | copy-start | bytes 388
  1.3 0.7 %copy-start.7 = (s32[1,1,1,128]{3,2,1,0:T(1,128)S(1)}, s32[1,1,1,128]{3,2,1,0:T(1,128)}, u32[]{:S(2)}) copy-start(s32[1,1,1,128]{3,2,1,0:T(1,128)} %ncount_any.1) | copy-start | bytes 1540
  1.3 0.7 %copy-start.8 = (f32[128]{0:T(128)S(1)}, f32[128]{0:T(128)}, u32[]{:S(2)}) copy-start(f32[128]{0:T(128)} %param.21) | copy-start | bytes 1540
  2.0 1.0 %copy-start = (f32[2,384,128]{2,1,0:T(8,128)S(1)}, f32[2,384,128]{2,1,0:T(8,128)}, u32[]{:S(2)}) copy-start(f32[2,384,128]{2,1,0:T(8,128)} %mix_any.1) | copy-start | bytes 1179652
  3.0 0.8 %copy-start.1 = (f32[2,64,128]{2,1,0:T(8,128)S(1)}, f32[2,64,128]{2,1,0:T(8,128)}, u32[]{:S(2)}) copy-start(f32[2,64,128]{2,1,0:T(8,128)} %w2_any.1) | copy-start | bytes 196612
  3.9 0.7 %copy-start.2 = (s32[1,1,1,32,128]{4,3,2,1,0:T(8,128)S(1)}, s32[1,1,1,32,128]{4,3,2,1,0:T(8,128)}, u32[]{:S(2)}) copy-start(s32[1,1,1,32,128]{4,3,2,1,0:T(8,128)} %send_any.1) | copy-start | bytes 49156
  4.6 0.7 %copy-start.3 = (f32[10,128]{1,0:T(8,128)S(1)}, f32[10,128]{1,0:T(8,128)}, u32[]{:S(2)}) copy-start(f32[10,128]{1,0:T(8,128)} %emb_any.1) | copy-start | bytes 15364
  5.3 0.7 %copy-start.4 = (f32[2,8,64]{2,1,0:T(8,128)S(1)}, f32[2,8,64]{2,1,0:T(8,128)}, u32[]{:S(2)}) copy-start(f32[2,8,64]{2,1,0:T(8,128)} %w1_any.1) | copy-start | bytes 12292

commit v2 on v1

--- a/solution.py
+++ b/solution.py
@@ -13,6 +13,8 @@
 GROUP = 4
 STEPS = NEIGH // GROUP
 WIDE = GROUP * ATOMS
+VMEM_BYTES = 64 * 1024 * 1024
+UNROLL = 4
 F32, BF16 = jnp.float32, jnp.bfloat16
 NN = (((1,), (0,)), ((), ()))
 NT = (((1,), (1,)), ((), ()))
@@ -118,7 +120,7 @@
     atom_row = lax.broadcasted_iota(jnp.int32, (ATOMS, ATOMS), 0)
     pick = (atom_row == brow).astype(F32)
     pick_t = pick.T
-    coords = pos_ref[0, 0, 0]
+    coords = pos_ref[0, 0, :, 0, :]
     kinds = spec_ref[0, 0].astype(F32)
     geo[...] = jnp.zeros_like(geo)
     geo[0:3, :] = coords
@@ -164,7 +166,7 @@
             oh[i, :, q * ATOMS : (q + 1) * ATOMS] = jnp.where(table_row == r, 1.0, 0.0).astype(BF16)
         return carry
 
-    lax.fori_loop(0, STEPS, build, 0)
+    lax.fori_loop(0, STEPS, build, 0, unroll=UNROLL)
 
     for name in ("emb", "w1", "w2", "count", "read", "mix"):
         loads[name].wait()
@@ -200,7 +202,7 @@
             gsc[i * GROUP + q] = lanes(x, q)
         return carry
 
-    lax.fori_loop(0, STEPS, gather_geo, 0)
+    lax.fori_loop(0, STEPS, gather_geo, 0, unroll=UNROLL)
 
     deltas = [(gsc[:, a, :] + off[a]) - coords[a : a + 1, :] for a in range(3)]
     dist = jnp.sqrt(deltas[0] * deltas[0] + deltas[1] * deltas[1] + deltas[2] * deltas[2] + 0.25)
@@ -254,7 +256,7 @@
                     msg[layer, i, :, q * ATOMS : (q + 1) * ATOMS] = f * lanes(r, q)
             return carry
 
-        lax.fori_loop(0, STEPS, step, 0)
+        lax.fori_loop(0, STEPS, step, 0, unroll=UNROLL)
 
     def density(layer):
         def step(cb, carry):
@@ -325,7 +327,7 @@
         msg[1, i] = f * rad[i]
         return carry
 
-    lax.fori_loop(0, STEPS, gather_h, 0)
+    lax.fori_loop(0, STEPS, gather_h, 0, unroll=UNROLL)
     z2 = density(1)
     sig2 = sigmoid(z2)
     final = h1 + z2 * sig2
@@ -373,7 +375,7 @@
             dr[i, :, cut] = dm * feat[1, i, :, cut]
         return carry
 
-    lax.fori_loop(0, STEPS, back_feat, 0)
+    lax.fori_loop(0, STEPS, back_feat, 0, unroll=UNROLL)
 
     dtab[...] = jnp.zeros_like(dtab)
 
@@ -381,7 +383,7 @@
         dtab[...] += lax.dot_general(oh[i], dg[i], NT, preferred_element_type=F32)
         return carry
 
-    lax.fori_loop(0, STEPS, scatter_h, 0)
+    lax.fori_loop(0, STEPS, scatter_h, 0, unroll=UNROLL)
     gtab[...] = dtab[:, 0:CH] + dtab[:, CH : 2 * CH]
     g_copies = [
         remote(
@@ -416,7 +418,7 @@
                     dbsum[i * GROUP + q] += lanes(db, q)
             return carry
 
-        lax.fori_loop(0, STEPS, step, 0)
+        lax.fori_loop(0, STEPS, step, 0, unroll=UNROLL)
 
     def back_sphere(i, carry):
         for q in range(GROUP):
@@ -426,7 +428,7 @@
                 dysum[k, pl.ds(i * GROUP + q, 1), :] = jnp.sum(m * dd[k], axis=0, keepdims=True)
         return carry
 
-    lax.fori_loop(0, STEPS, back_sphere, 0)
+    lax.fori_loop(0, STEPS, back_sphere, 0, unroll=UNROLL)
     back_radial(1, True)
     part = gathered(0, ex, e_copies)
     e_copies = spread(1, ey, ey_s, ey_r, part)
@@ -455,7 +457,7 @@
             dr[i, :, cut] = dm * feat[0, i, :, cut]
         return carry
 
-    lax.fori_loop(0, STEPS, back_first, 0)
+    lax.fori_loop(0, STEPS, back_first, 0, unroll=UNROLL)
     back_radial(0, False)
     part = gathered(1, ey, e_copies)
     e_copies = spread(2, ez, ez_s, ez_r, part)
@@ -480,7 +482,7 @@
         d = jnp.concatenate(split2(d), axis=0).astype(BF16)
         return carry + lax.dot_general(d, oh[i], NT, preferred_element_type=F32)
 
-    dxyz = lax.fori_loop(0, STEPS, scatter_geo, jnp.zeros((16, K), F32))
+    dxyz = lax.fori_loop(0, STEPS, scatter_geo, jnp.zeros((16, K), F32), unroll=UNROLL)
     dxyz = dxyz[0:8] + dxyz[8:16]
     for u in range(K // ATOMS):
         etile[u] = lanes(dxyz, u)
@@ -501,7 +503,7 @@
     r0, r1 = split2(ret)
     grad = etile[0] + (mm(r0, pick, NT) + mm(r1, pick, NT))
     for a in range(3):
-        force_ref[0, 0, 0, a : a + 1, :] = centre[a] - grad[a : a + 1, :]
+        force_ref[0, 0, a] = centre[a] - grad[a : a + 1, :]
 
 
 def on_device(
@@ -551,7 +553,7 @@
         vm((1 + T, 8, ATOMS), F32),
     ]
     operands = (
-        positions, species.reshape(1, 1, 1, ATOMS), atom_count.reshape(1, 1, 1, 1),
+        positions.reshape(1, 1, 3, 1, ATOMS), species.reshape(1, 1, 1, ATOMS), atom_count.reshape(1, 1, 1, 1),
         boundary.reshape(1, 1, 1, RIM), senders, neighbour_count.reshape(1, 1, 1, ATOMS),
         embed, radial_first, radial_second, mix, readout.reshape(1, CH),
     )
@@ -561,18 +563,18 @@
     forces, energy = pl.pallas_call(
         functools.partial(kernel, sizes),
         out_shape=(
-            jax.ShapeDtypeStruct((1, 1, 1, 3, ATOMS), F32),
+            jax.ShapeDtypeStruct((1, 1, 3, 1, ATOMS), F32),
             jax.ShapeDtypeStruct((1, ATOMS), F32),
         ),
         in_specs=[pl.BlockSpec(memory_space=pltpu.HBM)] * 11,
         out_specs=(pl.BlockSpec(memory_space=pltpu.VMEM),) * 2,
         scratch_shapes=scratch,
         compiler_params=pltpu.CompilerParams(
-            collective_id=0, has_side_effects=True, vmem_limit_bytes=50 * 1024 * 1024
+            collective_id=0, has_side_effects=True, vmem_limit_bytes=VMEM_BYTES
         ),
         name="brick",
     )(*operands)
-    return forces, energy[0, 0:1]
+    return forces.reshape(positions.shape), energy[0, 0:1]
 
 
 def solution(mesh):

time: 58.7 us -> 49.5 us (0.84)
  Pallas kernels: 50.6 us -> 45.5 us
  local copies, waits for them, and re-layouts: 5.19 us -> 1.29 us
    pallas_call x1, Pallas kernels: 50.6 us -> 45.5 us  [on_device(): pl.pallas_call(functools.partial(kernel, sizes), out_shape=(jax.ShapeDtyp...]
    unnamed x22 -> x5, local copies, waits for them, and re-layouts: 5.19 us -> 1.29 us
where the time goes in v2:
time: 49.5 us; the launch traced here: 49.3 us
  Pallas kernels  45.5 us (92%)
  between operations  2.46 us (5%)
  local copies, waits for them, and re-layouts  1.29 us (3%)
    pallas_call x1, Pallas kernels, on_device(): pl.pallas_call(functools.partial(kernel, sizes), out_shape=(jax.ShapeDtyp...  45.5 us
    unnamed x5, local copies, waits for them, and re-layouts  1.29 us

profile of v2, /device:TPU:0, one launch (start us, length us, event | category | flops | bytes accessed | tf_op | source)
XLA Modules:
  0.0 49.3 jit_solution(15463090633716271502)
XLA Ops:
  1.3 45.5 %brick.1 = (f32[1,1,3,1,128]{4,3,2,1,0:T(1,128)}, f32[1,128]{1,0:T(1,128)}) custom-call(f32[1,1,3,1,128]{4,3,2,1,0:T(1,128)} %bitcast.8, s32[1,1,1,128]{3,2,1,0:T(1,128)} %spec_any.1, s32[1,1,1,1]{3,2,1,0:T(1,128)S(6)} %copy.16.count_any, s32[1,1,1,32]{3,2,1,0:T(1,128)} %bound_any.1, s32[1,1,1,32,128]{4,3,2,1,0:T(8,128)} %send_any.1, ...), custom_call_target="tpu_custom_call" | custom-call | tf_op jit(solution)/shard_map/brick/pallas_call | solution.py:563
  46.8 0.0 copy-start
  46.8 0.7 %copy-done = f32[1,1,3,1,128]{4,3,2,1,0:T(1,128)S(1)} copy-done((f32[1,1,3,1,128]{4,3,2,1,0:T(1,128)S(1)}, f32[1,1,3,1,128]{4,3,2,1,0:T(1,128)}, u32[]{:S(2)}) %copy-start) | copy-done | bytes 1560
  47.5 0.0 copy-start.1
  47.5 0.6 %copy.17 = f32[1,1,1,3,128]{4,2,3,1,0:T(1,128)} copy(f32[1,1,1,3,128]{4,2,3,1,0:T(1,128)S(1)} %bitcast.7) | data formatting | bytes 3072
  48.0 0.1 copy-done.1
Async XLA Ops:
  46.8 0.7 %copy-start = (f32[1,1,3,1,128]{4,3,2,1,0:T(1,128)S(1)}, f32[1,1,3,1,128]{4,3,2,1,0:T(1,128)}, u32[]{:S(2)}) copy-start(f32[1,1,3,1,128]{4,3,2,1,0:T(1,128)} %get-tuple-element.4) | copy-start | bytes 4612
  47.5 0.6 %copy-start.1 = (f32[1,128]{1,0:T(1,128)S(1)}, f32[1,128]{1,0:T(1,128)}, u32[]{:S(2)}) copy-start(f32[1,128]{1,0:T(1,128)} %get-tuple-element.5) | copy-start | bytes 1540
